TPU v7x, 32 devices: a whole 2x2x4 slice. The times are simulated.
32 devices in a mesh: grp: 16 (over z, y, core), mem: 2 (over x).
Axes of the slice: x: 2, y: 2, z: 4, core: 2. Of those that a mesh axis runs over, the one named last changes fastest.
Arguments:
- features: bfloat16 [16384, 256], P(('grp', 'mem')), may hold values from -6 to 6
- initial: bfloat16 [16384, 256], P(('grp', 'mem')), may hold values from -6 to 6
- weight: bfloat16 [256, 256], replicated, may hold values from -0.375 to 0.375
- mask_in: int32 [16384, 512], P(('grp', 'mem')), may hold values 0 or 1
- mask_out: int32 [16384, 512], P(('grp', 'mem')), may hold values 0 or 1
- history: bfloat16 [32768, 256], P(('grp', 'mem')), may hold values from -6 to 6
- serve_rows: int32 [16384], P(('grp', 'mem')), may hold values from 0 to 1023, as said below
- push_rows: int32 [16384], P(('grp', 'mem')), may hold values from 0 to 1023, as said below
- cotangent: bfloat16 [16384, 256], P(('grp', 'mem')), may hold values from -6 to 6
Outputs:
- grad_weight: float32 [256, 256], replicated
- new_history: bfloat16 [32768, 256], P(('grp', 'mem'))
Inputs may be any that keep to these rules, and one draw needn't show every extreme that they name: `serve_rows`: the 512 entries of one partition are distinct local rows. `push_rows`: the 512 entries of one partition are distinct local rows.
All inputs are finite; a program needn't handle non-finite values. No bound on the sum of `mask_in` or of `mask_out` on one device may be relied on, other than what follows from the above.
Results may differ from a plain program's by a relative error of at most 0.005.
Values may be sent and summed in bfloat16 or wider, within the bound.
A program may use at most 64 MiB of HBM per device.

v0:
```python
import math

import jax
import jax.numpy as jnp
from jax import lax
from jax.sharding import PartitionSpec as P

ALPHA = 0.1
BETA = 0.5


def local(features, initial, weight, mask_in, mask_out, history, serve_rows, push_rows, cotangent):
    members = lax.axis_size("mem")
    batch = features.shape[0]
    pull = serve_rows.shape[0]
    width = features.shape[1]
    served = history[serve_rows].reshape(members, pull // members, width)
    pulled = lax.all_to_all(served, "mem", split_axis=0, concat_axis=0, tiled=True).reshape(
        pull, width
    )
    degree = (
        1.0
        + jnp.sum(mask_in, axis=1).astype(jnp.float32)
        + jnp.sum(mask_out, axis=1).astype(jnp.float32)
    )
    summed = features.astype(jnp.float32)
    summed = summed + jnp.dot(
        mask_in.astype(jnp.bfloat16), features, preferred_element_type=jnp.float32
    )
    summed = summed + jnp.dot(
        mask_out.astype(jnp.bfloat16), pulled, preferred_element_type=jnp.float32
    )
    summed = summed / degree[:, None]
    support = ((1.0 - ALPHA) * summed + ALPHA * initial.astype(jnp.float32)).astype(jnp.bfloat16)
    mixed = (1.0 - BETA) * support.astype(jnp.float32) + BETA * jnp.dot(
        support, weight, preferred_element_type=jnp.float32
    )
    sigma = jax.nn.sigmoid(mixed)
    embedded = (mixed * sigma).astype(jnp.bfloat16)
    delta = (cotangent.astype(jnp.float32) * sigma * (1.0 + mixed * (1.0 - sigma))).astype(
        jnp.bfloat16
    )
    pushed = lax.all_to_all(
        embedded.reshape(members, batch // members, width),
        "mem",
        split_axis=0,
        concat_axis=0,
        tiled=True,
    )
    new_history = history.at[push_rows].set(pushed.reshape(batch, width))
    factor = BETA / math.sqrt(lax.axis_size("grp") * members * batch)
    local_grad = factor * lax.dot_general(
        support, delta, (((0,), (0,)), ((), ())), preferred_element_type=jnp.float32
    )
    grad_weight = lax.psum(local_grad, ("grp", "mem"))
    return (grad_weight, new_history)


def solution(mesh):
    return jax.shard_map(
        local,
        mesh=mesh,
        in_specs=(
            P(("grp", "mem"), None),
            P(("grp", "mem"), None),
            P(),
            P(("grp", "mem"), None),
            P(("grp", "mem"), None),
            P(("grp", "mem"), None),
            P(("grp", "mem")),
            P(("grp", "mem")),
            P(("grp", "mem"), None),
        ),
        out_specs=(P(), P(("grp", "mem"), None)),
        check_vma=False,
    )
```

profile of v0, /device:TPU:0, one launch (start us, length us, event | category | flops | bytes accessed | tf_op | source)
XLA Modules:
  0.0 159.6 jit_solution(7706236783891179121)
XLA Ops:
  7.2 0.0 copy-start
  7.2 0.0 copy-start.5
  7.2 1.1 copy.16
  8.3 0.0 copy-done.5
  8.3 0.0 copy-start.2
  8.3 2.6 %gather_fusion = bf16[512,256]{1,0:T(8,128)(2,1)} fusion(bf16[1024,256]{1,0:T(8,128)(2,1)S(1)} %copy.16, s32[1024]{0:T(1024)S(1)} %pad_clamp_fusion), kind=kCustom, calls=%fused_computation | custom fusion | bytes 526336 | tf_op jit(solution)/shard_map/gather | solution.py:17
  10.9 4.3 %all-to-all-start = ((bf16[2,256,256]{2,1,0:T(8,128)(2,1)}), bf16[2,256,256]{2,1,0:T(8,128)(2,1)}, u32[]{:S(2)}, u32[]{:S(2)}) async-start(bf16[2,256,256]{2,1,0:T(8,128)(2,1)} %bitcast), calls=%async_computation | async-start | bytes 524288 | tf_op jit(solution)/shard_map/all_to_all | solution.py:18
  15.2 0.0 all-reduce.2.cloned.1.call-start
  15.2 0.0 copy-done.2
  15.2 0.0 copy-done.4
  15.2 0.3 convolution_add_fusion.1
  15.5 0.1 reduce_sum.18
  15.7 0.8 copy-done.3
  16.4 0.1 reduce_sum.19
  16.6 5.2 %all-to-all-done = bf16[2,256,256]{2,1,0:T(8,128)(2,1)} async-done(((bf16[2,256,256]{2,1,0:T(8,128)(2,1)}), bf16[2,256,256]{2,1,0:T(8,128)(2,1)}, u32[]{:S(2)}, u32[]{:S(2)}) %all-to-all-start) | async-done | bytes 262176 | tf_op jit(solution)/shard_map/all_to_all | solution.py:18
  21.9 0.0 copy-done.7
  21.9 1.3 fusion.5
  23.1 0.0 copy-done
  23.1 0.0 copy-start.8
  23.2 1.0 multiply_convert_fusion
  24.2 0.0 copy-done.8
  24.2 1.1 convolution_multiply_fusion
  25.3 0.0 all-reduce.2.cloned.1.call-update
  25.3 0.0 copy-start.6
  25.3 3.5 %all-to-all-start.1 = ((bf16[2,256,256]{2,1,0:T(8,128)(2,1)}), bf16[2,256,256]{2,1,0:T(8,128)(2,1)S(1)}, u32[]{:S(2)}, u32[]{:S(2)}) async-start(bf16[2,256,256]{2,1,0:T(8,128)(2,1)} %bitcast.3), calls=%async_computation.1 | async-start | bytes 524288 | tf_op jit(solution)/shard_map/all_to_all | solution.py:43
  28.8 0.0 copy-done.6
  28.8 5.3 %all-to-all-done.1 = bf16[2,256,256]{2,1,0:T(8,128)(2,1)S(1)} async-done(((bf16[2,256,256]{2,1,0:T(8,128)(2,1)}), bf16[2,256,256]{2,1,0:T(8,128)(2,1)S(1)}, u32[]{:S(2)}, u32[]{:S(2)}) %all-to-all-start.1) | async-done | bytes 262176 | tf_op jit(solution)/shard_map/all_to_all | solution.py:43
  34.1 2.6 %scatter_fusion = bf16[1024,256]{1,0:T(8,128)(2,1)S(1)} fusion(bf16[1024,256]{1,0:T(8,128)(2,1)S(1)} %copy.16, s32[512]{0:T(512)S(1)} %compare_select_fusion, bf16[512,256]{1,0:T(8,128)(2,1)S(1)} %bitcast.21), kind=kCustom, calls=%fused_computation.1 | custom fusion | bytes 788480 | tf_op jit(solution)/shard_map/scatter | solution.py:50
  36.8 0.0 copy-start.1
  36.8 114.3 %all-reduce.2.cloned.1.call-done = f32[256,256]{1,0:T(8,128)} async-done(((f32[256,256]{1,0:T(8,128)}), f32[256,256]{1,0:T(8,128)}) %all-reduce.2.cloned.1.call-update) | async-done | bytes 262160 | tf_op jit(solution)/shard_map/psum | solution.py:55
  151.0 1.7 %copy.17 = f32[256,256]{1,0:T(8,128)} copy(f32[256,256]{1,0:T(8,128)} %all-reduce.2.cloned.1.call-done) | data formatting | bytes 524288
  152.7 0.0 copy-done.1
  (7 shorter events, 0.0 us)
Async XLA Ops:
  7.2 16.0 %copy-start = (bf16[256,256]{1,0:T(8,128)(2,1)S(1)}, bf16[256,256]{1,0:T(8,128)(2,1)}, u32[]{:S(2)}) copy-start(bf16[256,256]{1,0:T(8,128)(2,1)} %param.11) | copy-start | bytes 393220
  7.2 1.1 copy-start.5
  8.3 6.9 %copy-start.2 = (s32[512,512]{1,0:T(8,128)S(1)}, s32[512,512]{1,0:T(8,128)}, u32[]{:S(2)}) copy-start(s32[512,512]{1,0:T(8,128)} %param.12) | copy-start | bytes 3145732
  10.9 4.3 %copy-start.4 = (bf16[512,256]{1,0:T(8,128)(2,1)S(1)}, bf16[512,256]{1,0:T(8,128)(2,1)}, u32[]{:S(2)}) copy-start(bf16[512,256]{1,0:T(8,128)(2,1)} %param.9) | copy-start | bytes 786436
  10.9 11.0 %all-to-all-start = ((bf16[2,256,256]{2,1,0:T(8,128)(2,1)}), bf16[2,256,256]{2,1,0:T(8,128)(2,1)}, u32[]{:S(2)}, u32[]{:S(2)}) async-start(bf16[2,256,256]{2,1,0:T(8,128)(2,1)} %bitcast), calls=%async_computation | async-start | bytes 524288 | tf_op jit(solution)/shard_map/all_to_all | solution.py:18
  15.2 1.2 copy-start.3
  15.2 135.8 %all-reduce.2.cloned.1.call-start = ((), (), s32[]{:S(2)}) async-start(), calls=%async_computation.2 | async-start | bytes 524288 | tf_op jit(solution)/shard_map/psum | solution.py:55
  16.4 5.4 %copy-start.7 = (bf16[512,256]{1,0:T(8,128)(2,1)S(1)}, bf16[512,256]{1,0:T(8,128)(2,1)}, u32[]{:S(2)}) copy-start(bf16[512,256]{1,0:T(8,128)(2,1)} %param.10) | copy-start | bytes 786436
  23.1 1.1 copy-start.8
  25.3 3.5 %copy-start.6 = (s32[512]{0:T(512)S(1)}, s32[512]{0:T(512)}, u32[]{:S(2)}) copy-start(s32[512]{0:T(512)} %param.16) | copy-start | bytes 6148
  25.3 8.8 %all-to-all-start.1 = ((bf16[2,256,256]{2,1,0:T(8,128)(2,1)}), bf16[2,256,256]{2,1,0:T(8,128)(2,1)S(1)}, u32[]{:S(2)}, u32[]{:S(2)}) async-start(bf16[2,256,256]{2,1,0:T(8,128)(2,1)} %bitcast.3), calls=%async_computation.1 | async-start | bytes 524288 | tf_op jit(solution)/shard_map/all_to_all | solution.py:43
  36.8 115.9 %copy-start.1 = (bf16[1024,256]{1,0:T(8,128)(2,1)}, bf16[1024,256]{1,0:T(8,128)(2,1)S(1)}, u32[]{:S(2)}) copy-start(bf16[1024,256]{1,0:T(8,128)(2,1)S(1)} %scatter_fusion) | copy-start | bytes 1572868
Sparse Core Ops, SparseCore 0:
  25.5 125.5 all-reduce.1
where the time goes:
time: 160 us
  waiting for transfers between devices  125 us (78%)
  between operations  14.1 us (9%)
  local copies, waits for them, and re-layouts  8.74 us (5%)
  starting transfers between devices  7.79 us (5%)
  matrix products  3.71 us (2%)
    psum x1, waiting for transfers between devices, local(): grad_weight = lax.psum(local_grad, ('grp', 'mem'))  114 us
    all_to_all x1, waiting for transfers between devices, local(): lax.all_to_all(embedded.reshape(members, batch // members, width), 'mem',...  5.31 us
    all_to_all x1, waiting for transfers between devices, local(): lax.all_to_all(served, 'mem', split_axis=0, concat_axis=0, tiled=True)  5.25 us
    all_to_all x1, starting transfers between devices, local(): lax.all_to_all(served, 'mem', split_axis=0, concat_axis=0, tiled=True)  4.34 us
    unnamed x20, local copies, waits for them, and re-layouts  3.56 us
    all_to_all x1, starting transfers between devices, local(): lax.all_to_all(embedded.reshape(members, batch // members, width), 'mem',...  3.46 us
  transfers between devices with their start and end apart: 3, of which 3 were waited for; matrix products, arithmetic and copies ran while one was open for 2% of the time, Pallas kernels for 0%

commit v1 on v0

v1 whole, which is shorter than its diff:
```python
import functools
import math

import jax
import jax.numpy as jnp
from jax import lax
from jax.experimental import pallas as pl
from jax.experimental.pallas import tpu as pltpu
from jax.sharding import PartitionSpec as P

ALPHA = 0.1
BETA = 0.5
F32 = jnp.float32
BF16 = jnp.bfloat16
MESH = pl.DeviceIdType.MESH


def dot(a, b, contract=((1,), (0,))):
    return lax.dot_general(a, b, (contract, ((), ())), preferred_element_type=F32)


def kernel(
    groups,
    members,
    low,
    factor,
    features_in,
    initial_in,
    weight_in,
    mask_in_in,
    mask_out_in,
    history_in,
    serve_in,
    push_in,
    cotangent_in,
    grad_out,
    history_out,
    features,
    initial,
    weight,
    mask_in,
    mask_out,
    history,
    serve,
    push,
    cotangent,
    served,
    pulled,
    embedded,
    pushed,
    base,
    table,
    part,
    parts,
    chunk,
    chunks,
    final,
    finals,
    total,
    load_sem,
    store_sem,
    pull_send,
    pull_recv,
    push_send,
    push_recv,
    part_send,
    part_recv,
    chunk_send,
    chunk_recv,
    final_send,
    final_recv,
):
    g = lax.axis_index("grp")
    m = lax.axis_index("mem")
    batch, width = features.shape
    pull = serve.shape[1]
    rows = history.shape[0]
    k = pull // members
    q = batch // members
    plane = low * members
    planes = groups // low
    high = g // low
    inner = g % low
    spot = inner * members + m
    depth = width // plane

    def at_spot(p):
        return (high * low + p // members, p % members)

    def at_plane(h):
        return (h * low + inner, m)

    barrier = pltpu.get_barrier_semaphore()
    for off in range(1, plane):
        pl.semaphore_signal(
            barrier, inc=1, device_id=at_spot((spot + off) % plane), device_id_type=MESH
        )
    for off in range(1, planes):
        pl.semaphore_signal(
            barrier, inc=1, device_id=at_plane((high + off) % planes), device_id_type=MESH
        )

    loads = {}
    for i, (name, src, dst) in enumerate(
        (
            ("serve", serve_in, serve),
            ("history", history_in, history),
            ("push", push_in, push),
            ("features", features_in, features),
            ("mask_in", mask_in_in, mask_in),
            ("mask_out", mask_out_in, mask_out),
            ("initial", initial_in, initial),
            ("weight", weight_in, weight),
            ("cotangent", cotangent_in, cotangent),
        )
    ):
        loads[name] = pltpu.make_async_copy(src, dst, load_sem.at[i])
        loads[name].start()

    loads["serve"].wait()
    loads["history"].wait()

    def gather(j):
        wanted = serve[:, pl.ds(pl.multiple_of(j * k, 128), k)]
        wanted = jnp.transpose(jnp.broadcast_to(wanted, (128, k)))
        lane = lax.broadcasted_iota(jnp.int32, (k, 128), 1)
        found = dot(
            jnp.concatenate(
                [
                    jnp.where(wanted == lane + 128 * i, 1.0, 0.0).astype(BF16)
                    for i in range(rows // 128)
                ],
                axis=1,
            ),
            history[...],
        )
        return found.astype(BF16)

    for off in range(1, members):
        j = (m + off) % members
        served[off - 1] = gather(j)

    pl.semaphore_wait(barrier, plane - 1 + planes - 1)
    pulls = []
    for off in range(1, members):
        j = (m + off) % members
        copy = pltpu.make_async_remote_copy(
            src_ref=served.at[off - 1],
            dst_ref=pulled.at[off - 1],
            send_sem=pull_send.at[off - 1],
            recv_sem=pull_recv.at[off - 1],
            device_id=(g, j),
            device_id_type=MESH,
        )
        copy.start()
        pulls.append(copy)

    own = gather(m)
    loads["features"].wait()
    loads["mask_in"].wait()
    loads["mask_out"].wait()
    summed = features[...].astype(F32) + dot(
        mask_in[...].astype(F32).astype(BF16), features[...]
    )
    degree = 1.0 + jnp.sum(
        (mask_in[...] + mask_out[...]).astype(F32), axis=1, keepdims=True
    )
    inverse = 1.0 / degree

    def columns(j):
        return (
            mask_out[:, pl.ds(pl.multiple_of(j * k, 128), k)].astype(F32).astype(BF16)
        )

    summed = summed + dot(columns(m), own)

    loads["push"].wait()
    loads["initial"].wait()
    loads["weight"].wait()
    loads["cotangent"].wait()

    def hot(j):
        targets = push[:, pl.ds(pl.multiple_of(j * q, 128), q)]
        row = lax.broadcasted_iota(jnp.int32, (rows, q), 0)
        return jnp.where(row == targets, 1.0, 0.0).astype(BF16)

    row = lax.broadcasted_iota(jnp.int32, (rows, batch), 0)
    marks = jnp.where(row == push[...], 1.0, 0.0).astype(BF16)
    covered = dot(marks, jnp.ones((batch, 128), BF16))
    covered = jnp.concatenate([covered] * (width // 128), axis=1)
    base[...] = jnp.where(covered > 0.5, 0.0, history[...].astype(F32))

    for off in range(1, members):
        j = (m - off + members) % members
        pulls[off - 1].wait_recv()
        summed = summed + dot(columns(j), pulled[off - 1])

    support = (
        (1.0 - ALPHA) * (summed * inverse) + ALPHA * initial[...].astype(F32)
    ).astype(BF16)
    mixed = (1.0 - BETA) * support.astype(F32) + BETA * dot(support, weight[...])
    sigma = jax.nn.sigmoid(mixed)
    embedded[...] = (mixed * sigma).astype(BF16)
    delta = (
        cotangent[...].astype(F32) * sigma * (1.0 + mixed * (1.0 - sigma))
    ).astype(BF16)
    partial = factor * dot(support, delta, ((0,), (0,)))
    part[...] = partial.astype(part.dtype)

    sends = []
    for off in range(1, plane):
        p = (spot + off) % plane
        copy = pltpu.make_async_remote_copy(
            src_ref=part.at[pl.ds(pl.multiple_of(p * depth, depth), depth)],
            dst_ref=parts.at[off - 1],
            send_sem=part_send.at[off - 1],
            recv_sem=part_recv.at[off - 1],
            device_id=at_spot(p),
            device_id_type=MESH,
        )
        copy.start()
        sends.append(copy)

    pushes = []
    for off in range(1, members):
        j = (m + off) % members
        copy = pltpu.make_async_remote_copy(
            src_ref=embedded.at[pl.ds(pl.multiple_of(j * q, q), q)],
            dst_ref=pushed.at[off - 1],
            send_sem=push_send.at[off - 1],
            recv_sem=push_recv.at[off - 1],
            device_id=(g, j),
            device_id_type=MESH,
        )
        copy.start()
        pushes.append(copy)

    base[...] += dot(hot(m), embedded[pl.ds(pl.multiple_of(m * q, q), q), :])

    mine = part[pl.ds(pl.multiple_of(spot * depth, depth), depth), :].astype(F32)
    for off in range(1, plane):
        sends[off - 1].wait_recv()
        mine = mine + parts[off - 1].astype(F32)
    chunk[...] = mine.astype(chunk.dtype)
    chunks[high] = chunk[...]
    rounds = []
    for off in range(1, planes):
        h = (high + off) % planes
        copy = pltpu.make_async_remote_copy(
            src_ref=chunk,
            dst_ref=chunks.at[high],
            send_sem=chunk_send.at[off - 1],
            recv_sem=chunk_recv.at[off - 1],
            device_id=at_plane(h),
            device_id_type=MESH,
        )
        copy.start()
        rounds.append(copy)

    fresh = base[...]
    for off in range(1, members):
        j = (m - off + members) % members
        pushes[off - 1].wait_recv()
        fresh = fresh + dot(hot(j), pushed[off - 1])
    table[...] = fresh.astype(BF16)
    store = pltpu.make_async_copy(table, history_out, store_sem.at[0])
    store.start()

    for copy in rounds:
        copy.wait_recv()
    whole = chunks[0].astype(F32)
    for h in range(1, planes):
        whole = whole + chunks[h].astype(F32)
    final[...] = whole.astype(final.dtype)
    finals[spot] = final[...]
    lasts = []
    for off in range(1, plane):
        p = (spot + off) % plane
        copy = pltpu.make_async_remote_copy(
            src_ref=final,
            dst_ref=finals.at[spot],
            send_sem=final_send.at[off - 1],
            recv_sem=final_recv.at[off - 1],
            device_id=at_spot(p),
            device_id_type=MESH,
        )
        copy.start()
        lasts.append(copy)
    for copy in lasts:
        copy.wait_recv()
    total[...] = finals[...].astype(F32).reshape(width, width)
    write = pltpu.make_async_copy(total, grad_out, store_sem.at[1])
    write.start()
    for copy in pulls + sends + pushes + rounds + lasts:
        copy.wait_send()
    store.wait()
    write.wait()


def local(
    groups,
    members,
    features,
    initial,
    weight,
    mask_in,
    mask_out,
    history,
    serve_rows,
    push_rows,
    cotangent,
):
    batch, width = features.shape
    pull = serve_rows.shape[0]
    rows = history.shape[0]
    low = max(1, 8 // members)
    while groups % low:
        low -= 1
    plane = low * members
    planes = groups // low
    depth = width // plane
    wire = BF16
    factor = BETA / math.sqrt(groups * members * batch)
    vmem = pltpu.VMEM
    dma = pltpu.SemaphoreType.DMA
    anywhere = pl.BlockSpec(memory_space=pl.ANY)
    return pl.pallas_call(
        functools.partial(kernel, groups, members, low, factor),
        out_shape=(
            jax.ShapeDtypeStruct((width, width), F32),
            jax.ShapeDtypeStruct((rows, width), BF16),
        ),
        in_specs=[anywhere] * 9,
        out_specs=(anywhere, anywhere),
        scratch_shapes=[
            vmem(features.shape, BF16),
            vmem(initial.shape, BF16),
            vmem(weight.shape, BF16),
            vmem(mask_in.shape, jnp.int32),
            vmem(mask_out.shape, jnp.int32),
            vmem(history.shape, BF16),
            vmem((1, pull), jnp.int32),
            vmem((1, batch), jnp.int32),
            vmem(cotangent.shape, BF16),
            vmem((members - 1, pull // members, width), BF16),
            vmem((members - 1, pull // members, width), BF16),
            vmem((batch, width), BF16),
            vmem((members - 1, batch // members, width), BF16),
            vmem((rows, width), F32),
            vmem((rows, width), BF16),
            vmem((width, width), wire),
            vmem((plane - 1, depth, width), wire),
            vmem((depth, width), wire),
            vmem((planes, depth, width), wire),
            vmem((depth, width), wire),
            vmem((plane, depth, width), wire),
            vmem((width, width), F32),
            dma((9,)),
            dma((2,)),
            dma((members - 1,)),
            dma((members - 1,)),
            dma((members - 1,)),
            dma((members - 1,)),
            dma((plane - 1,)),
            dma((plane - 1,)),
            dma((planes - 1,)),
            dma((planes - 1,)),
            dma((plane - 1,)),
            dma((plane - 1,)),
        ],
        compiler_params=pltpu.CompilerParams(
            collective_id=0, has_side_effects=True, vmem_limit_bytes=60 * 1024 * 1024
        ),
    )(
        features,
        initial,
        weight,
        mask_in,
        mask_out,
        history,
        serve_rows.reshape(1, pull),
        push_rows.reshape(1, batch),
        cotangent,
    )


def solution(mesh):
    groups = mesh.shape["grp"]
    members = mesh.shape["mem"]
    split = P(("grp", "mem"), None)
    return jax.shard_map(
        functools.partial(local, groups, members),
        mesh=mesh,
        in_specs=(split, split, P(), split, split, split, P(("grp", "mem")), P(("grp", "mem")), split),
        out_specs=(P(), split),
        check_vma=False,
    )
```

time: 160 us -> 26.6 us (0.17)
  waiting for transfers between devices: 125 us -> 0 us
  Pallas kernels: 0 us -> 23.2 us
  between operations: 14.1 us -> 0.65 us
  starting transfers between devices: 7.79 us -> 0 us
  local copies, waits for them, and re-layouts: 8.74 us -> 2.52 us
  matrix products: 3.71 us -> 0 us
    psum x1 -> x0, waiting for transfers between devices: 114 us -> none  [local(): grad_weight = lax.psum(local_grad, ('grp', 'mem'))]
    pallas_call x0 -> x1, Pallas kernels: none -> 23.2 us  [local(): pl.pallas_call(functools.partial(kernel, groups, members, low, factor), o...]
    all_to_all x2 -> x0, waiting for transfers between devices: 10.6 us -> none  [the longest x1 5.31 us: local(): lax.all_to_all(embedded.reshape(members, batch // members, width), 'mem',...]
    all_to_all x2 -> x0, starting transfers between devices: 7.79 us -> none  [the longest x1 4.34 us: local(): lax.all_to_all(served, 'mem', split_axis=0, concat_axis=0, tiled=True)]
    dot_general x4 -> x0, matrix products: 3.71 us -> none  [the longest x1 1.26 us: local(): jnp.dot(mask_out.astype(jnp.bfloat16), pulled, preferred_element_type=jnp...]
    scatter x1 -> x0, local copies, waits for them, and re-layouts: 2.61 us -> none  [local(): new_history = history.at[push_rows].set(pushed.reshape(batch, width))]
    gather x1 -> x0, local copies, waits for them, and re-layouts: 2.58 us -> none  [local(): served = history[serve_rows].reshape(members, pull // members, width)]
    unnamed x20 -> x4, local copies, waits for them, and re-layouts: 3.56 us -> 2.52 us
  transfers between devices with their start and end apart: 3 -> 0, of which waited for: 3 -> 0; matrix products, arithmetic and copies ran while one was open for 2% -> 0% of each run, Pallas kernels for 0% -> 0%
where the time goes in v1:
time: 26.6 us; the launch traced here: 26.4 us
  Pallas kernels  23.2 us (87%)
  local copies, waits for them, and re-layouts  2.52 us (9%)
  between operations  0.65 us (2%)
    pallas_call x1, Pallas kernels, local(): pl.pallas_call(functools.partial(kernel, groups, members, low, factor), o...  23.2 us
    unnamed x4, local copies, waits for them, and re-layouts  2.52 us

profile of v1, /device:TPU:0, one launch (start us, length us, event | category | flops | bytes accessed | tf_op | source)
XLA Modules:
  0.0 26.4 jit_solution(11945643031838883014)
XLA Ops:
  0.6 23.2 %shard_map.104 = (f32[256,256]{1,0:T(8,128)}, bf16[1024,256]{1,0:T(8,128)(2,1)}) custom-call(bf16[512,256]{1,0:T(8,128)(2,1)} %features_in.1, bf16[512,256]{1,0:T(8,128)(2,1)} %initial_in.1, bf16[256,256]{1,0:T(8,128)(2,1)} %weight_in.1, s32[512,512]{1,0:T(8,128)} %mask_in_in.1, s32[512,512]{1,0:T(8,128)} %mask_out_in.1, bf16[1024,256]{1,0:T(8,128)(2,1)} %history_in.1, ...), custom_call_target="tpu_custom_call" | custom-call | tf_op jit(solution)/shard_map/pallas_call | solution.py:327
  23.9 0.0 copy-start
  23.9 1.7 %copy.13 = f32[256,256]{1,0:T(8,128)} copy(f32[256,256]{1,0:T(8,128)} %get-tuple-element.4) | data formatting | bytes 524288
  25.6 0.0 copy-done
  25.6 0.8 %copy.14 = bf16[1024,256]{1,0:T(8,128)(2,1)} copy(bf16[1024,256]{1,0:T(8,128)(2,1)S(1)} %copy-done) | data formatting | bytes 1048576
Async XLA Ops:
  23.9 1.7 %copy-start = (bf16[1024,256]{1,0:T(8,128)(2,1)S(1)}, bf16[1024,256]{1,0:T(8,128)(2,1)}, u32[]{:S(2)}) copy-start(bf16[1024,256]{1,0:T(8,128)(2,1)} %get-tuple-element.5) | copy-start | bytes 1572868

commit v2 on v1

--- a/solution.py
+++ b/solution.py
@@ -10,6 +10,7 @@
 
 ALPHA = 0.1
 BETA = 0.5
+BLOCK = 256
 F32 = jnp.float32
 BF16 = jnp.bfloat16
 MESH = pl.DeviceIdType.MESH
@@ -49,16 +50,18 @@
     embedded,
     pushed,
     base,
-    table,
+    known,
+    scale,
+    others,
     part,
     parts,
     chunk,
     chunks,
     final,
     finals,
-    total,
     load_sem,
-    store_sem,
+    corner_sem,
+    line_sem,
     pull_send,
     pull_recv,
     push_send,
@@ -83,22 +86,55 @@
     inner = g % low
     spot = inner * members + m
     depth = width // plane
-
-    def at_spot(p):
-        return (high * low + p // members, p % members)
+    block = min(batch, BLOCK)
+    blocks = [pl.ds(i, block) for i in range(0, batch, block)]
 
     def at_plane(h):
         return (h * low + inner, m)
 
+    offsets = [
+        (di, dm) for di in range(low) for dm in range(members) if di or dm
+    ]
+    offsets.sort(key=lambda o: -((o[0] > 0) + (o[1] > 0)))
+
+    def shifted(di, dm):
+        return (high * low + (inner + di) % low, (m + dm) % members)
+
+    chained = 2 < planes <= 4
     barrier = pltpu.get_barrier_semaphore()
-    for off in range(1, plane):
-        pl.semaphore_signal(
-            barrier, inc=1, device_id=at_spot((spot + off) % plane), device_id_type=MESH
-        )
-    for off in range(1, planes):
-        pl.semaphore_signal(
-            barrier, inc=1, device_id=at_plane((high + off) % planes), device_id_type=MESH
-        )
+
+    def signal(semaphore, device):
+        pl.semaphore_signal(semaphore, inc=1, device_id=device, device_id_type=MESH)
+
+    near = [o for o in offsets if 0 in o]
+    for di, dm in near:
+        signal(barrier, shifted(di, dm))
+    if chained:
+
+        def along(semaphores):
+            @pl.when(high > 0)
+            def _():
+                signal(semaphores[0], at_plane(high - 1))
+
+            @pl.when(high < planes - 1)
+            def _():
+                signal(semaphores[1], at_plane(high + 1))
+
+        def heard(semaphores):
+            @pl.when(high < planes - 1)
+            def _():
+                pl.semaphore_wait(semaphores[0], 1)
+
+            @pl.when(high > 0)
+            def _():
+                pl.semaphore_wait(semaphores[1], 1)
+
+        along((barrier, barrier))
+        beside = (high > 0).astype(jnp.int32) + (high < planes - 1).astype(jnp.int32)
+    else:
+        for off in range(1, planes):
+            signal(barrier, at_plane((high + off) % planes))
+        beside = planes - 1
 
     loads = {}
     for i, (name, src, dst) in enumerate(
@@ -140,7 +176,7 @@
         j = (m + off) % members
         served[off - 1] = gather(j)
 
-    pl.semaphore_wait(barrier, plane - 1 + planes - 1)
+    pl.semaphore_wait(barrier, len(near) + beside)
     pulls = []
     for off in range(1, members):
         j = (m + off) % members
@@ -154,72 +190,113 @@
         )
         copy.start()
         pulls.append(copy)
+    for di in range(1, low):
+        signal(corner_sem, shifted(di, 0))
+    if chained:
+        along((line_sem.at[0, 0], line_sem.at[0, 1]))
 
     own = gather(m)
     loads["features"].wait()
     loads["mask_in"].wait()
     loads["mask_out"].wait()
-    summed = features[...].astype(F32) + dot(
-        mask_in[...].astype(F32).astype(BF16), features[...]
-    )
-    degree = 1.0 + jnp.sum(
-        (mask_in[...] + mask_out[...]).astype(F32), axis=1, keepdims=True
-    )
-    inverse = 1.0 / degree
-
-    def columns(j):
+    loads["initial"].wait()
+
+    def columns(j, rows_at):
         return (
-            mask_out[:, pl.ds(pl.multiple_of(j * k, 128), k)].astype(F32).astype(BF16)
-        )
-
-    summed = summed + dot(columns(m), own)
-
-    loads["push"].wait()
-    loads["initial"].wait()
+            mask_out[rows_at, pl.ds(pl.multiple_of(j * k, 128), k)]
+            .astype(F32)
+            .astype(BF16)
+        )
+
+    for at in blocks:
+        summed = features[at, :].astype(F32)
+        summed = summed + dot(mask_in[at, :].astype(F32).astype(BF16), features[...])
+        summed = summed + dot(columns(m, at), own)
+        degree = 1.0 + jnp.sum(
+            (mask_in[at, :] + mask_out[at, :]).astype(F32), axis=1, keepdims=True
+        )
+        share = jnp.broadcast_to((1.0 - ALPHA) / degree, (block, width))
+        scale[at, :] = share
+        known[at, :] = share * summed + ALPHA * initial[at, :].astype(F32)
+        for off in range(1, members):
+            others[off - 1, at, :] = columns((m - off + members) % members, at)
+
     loads["weight"].wait()
     loads["cotangent"].wait()
+    if chained:
+        heard((line_sem.at[0, 0], line_sem.at[0, 1]))
+        along((line_sem.at[1, 0], line_sem.at[1, 1]))
+
+    for copy in pulls:
+        copy.wait_recv()
+    partial = None
+    for at in blocks:
+        extra = dot(others[0, at, :], pulled[0])
+        for off in range(2, members):
+            extra = extra + dot(others[off - 1, at, :], pulled[off - 1])
+        support = (known[at, :] + scale[at, :] * extra).astype(BF16)
+        mixed = (1.0 - BETA) * support.astype(F32) + BETA * dot(support, weight[...])
+        sigma = 0.5 + 0.5 * jnp.tanh(0.5 * mixed)
+        embedded[at, :] = (mixed * sigma).astype(BF16)
+        delta = (
+            cotangent[at, :].astype(F32) * sigma * (1.0 + mixed * (1.0 - sigma))
+        ).astype(BF16)
+        term = dot(support, delta, ((0,), (0,)))
+        partial = term if partial is None else partial + term
+    part[...] = (factor * partial).astype(part.dtype)
+    if low > 1:
+        pl.semaphore_wait(corner_sem, low - 1)
+
+    sends = []
+    for i, (di, dm) in enumerate(offsets):
+        p = (inner + di) % low * members + (m + dm) % members
+        copy = pltpu.make_async_remote_copy(
+            src_ref=part.at[pl.ds(pl.multiple_of(p * depth, depth), depth)],
+            dst_ref=parts.at[i],
+            send_sem=part_send.at[i],
+            recv_sem=part_recv.at[i],
+            device_id=shifted(di, dm),
+            device_id_type=MESH,
+        )
+        copy.start()
+        sends.append(copy)
+
+    loads["push"].wait()
 
     def hot(j):
         targets = push[:, pl.ds(pl.multiple_of(j * q, 128), q)]
         row = lax.broadcasted_iota(jnp.int32, (rows, q), 0)
         return jnp.where(row == targets, 1.0, 0.0).astype(BF16)
 
-    row = lax.broadcasted_iota(jnp.int32, (rows, batch), 0)
-    marks = jnp.where(row == push[...], 1.0, 0.0).astype(BF16)
-    covered = dot(marks, jnp.ones((batch, 128), BF16))
+    covered = dot(hot(0), jnp.ones((q, 128), BF16))
+    for j in range(1, members):
+        covered = covered + dot(hot(j), jnp.ones((q, 128), BF16))
     covered = jnp.concatenate([covered] * (width // 128), axis=1)
-    base[...] = jnp.where(covered > 0.5, 0.0, history[...].astype(F32))
-
-    for off in range(1, members):
-        j = (m - off + members) % members
-        pulls[off - 1].wait_recv()
-        summed = summed + dot(columns(j), pulled[off - 1])
-
-    support = (
-        (1.0 - ALPHA) * (summed * inverse) + ALPHA * initial[...].astype(F32)
-    ).astype(BF16)
-    mixed = (1.0 - BETA) * support.astype(F32) + BETA * dot(support, weight[...])
-    sigma = jax.nn.sigmoid(mixed)
-    embedded[...] = (mixed * sigma).astype(BF16)
-    delta = (
-        cotangent[...].astype(F32) * sigma * (1.0 + mixed * (1.0 - sigma))
-    ).astype(BF16)
-    partial = factor * dot(support, delta, ((0,), (0,)))
-    part[...] = partial.astype(part.dtype)
-
-    sends = []
+    base[...] = jnp.where(covered > 0.5, 0.0, history[...].astype(F32)) + dot(
+        hot(m), embedded[pl.ds(pl.multiple_of(m * q, q), q), :]
+    )
+
+    mine = part[pl.ds(pl.multiple_of(spot * depth, depth), depth), :].astype(F32)
     for off in range(1, plane):
-        p = (spot + off) % plane
+        sends[off - 1].wait_recv()
+        mine = mine + parts[off - 1].astype(F32)
+    chunk[...] = mine.astype(chunk.dtype)
+    chunks[high] = chunk[...]
+    if chained:
+        heard((line_sem.at[1, 0], line_sem.at[1, 1]))
+    rounds = []
+    for off in range(1, planes):
+        h = (high + off) % planes
         copy = pltpu.make_async_remote_copy(
-            src_ref=part.at[pl.ds(pl.multiple_of(p * depth, depth), depth)],
-            dst_ref=parts.at[off - 1],
-            send_sem=part_send.at[off - 1],
-            recv_sem=part_recv.at[off - 1],
-            device_id=at_spot(p),
+            src_ref=chunk,
+            dst_ref=chunks.at[high],
+            send_sem=chunk_send.at[off - 1],
+            recv_sem=chunk_recv.at[off - 1],
+            device_id=at_plane(h),
             device_id_type=MESH,
         )
         copy.start()
-        sends.append(copy)
+        rounds.append(copy)
 
     pushes = []
     for off in range(1, members):
@@ -235,37 +312,6 @@
         copy.start()
         pushes.append(copy)
 
-    base[...] += dot(hot(m), embedded[pl.ds(pl.multiple_of(m * q, q), q), :])
-
-    mine = part[pl.ds(pl.multiple_of(spot * depth, depth), depth), :].astype(F32)
-    for off in range(1, plane):
-        sends[off - 1].wait_recv()
-        mine = mine + parts[off - 1].astype(F32)
-    chunk[...] = mine.astype(chunk.dtype)
-    chunks[high] = chunk[...]
-    rounds = []
-    for off in range(1, planes):
-        h = (high + off) % planes
-        copy = pltpu.make_async_remote_copy(
-            src_ref=chunk,
-            dst_ref=chunks.at[high],
-            send_sem=chunk_send.at[off - 1],
-            recv_sem=chunk_recv.at[off - 1],
-            device_id=at_plane(h),
-            device_id_type=MESH,
-        )
-        copy.start()
-        rounds.append(copy)
-
-    fresh = base[...]
-    for off in range(1, members):
-        j = (m - off + members) % members
-        pushes[off - 1].wait_recv()
-        fresh = fresh + dot(hot(j), pushed[off - 1])
-    table[...] = fresh.astype(BF16)
-    store = pltpu.make_async_copy(table, history_out, store_sem.at[0])
-    store.start()
-
     for copy in rounds:
         copy.wait_recv()
     whole = chunks[0].astype(F32)
@@ -274,27 +320,29 @@
     final[...] = whole.astype(final.dtype)
     finals[spot] = final[...]
     lasts = []
-    for off in range(1, plane):
-        p = (spot + off) % plane
+    for i, (di, dm) in enumerate(offsets):
         copy = pltpu.make_async_remote_copy(
             src_ref=final,
             dst_ref=finals.at[spot],
-            send_sem=final_send.at[off - 1],
-            recv_sem=final_recv.at[off - 1],
-            device_id=at_spot(p),
+            send_sem=final_send.at[i],
+            recv_sem=final_recv.at[i],
+            device_id=shifted(di, dm),
             device_id_type=MESH,
         )
         copy.start()
         lasts.append(copy)
+    fresh = base[...]
+    for off in range(1, members):
+        j = (m - off + members) % members
+        pushes[off - 1].wait_recv()
+        fresh = fresh + dot(hot(j), pushed[off - 1])
+    history_out[...] = fresh.astype(BF16)
+
     for copy in lasts:
         copy.wait_recv()
-    total[...] = finals[...].astype(F32).reshape(width, width)
-    write = pltpu.make_async_copy(total, grad_out, store_sem.at[1])
-    write.start()
+    grad_out[...] = finals[...].astype(F32).reshape(width, width)
     for copy in pulls + sends + pushes + rounds + lasts:
         copy.wait_send()
-    store.wait()
-    write.wait()
 
 
 def local(
@@ -327,11 +375,11 @@
     return pl.pallas_call(
         functools.partial(kernel, groups, members, low, factor),
         out_shape=(
-            jax.ShapeDtypeStruct((width, width), F32),
-            jax.ShapeDtypeStruct((rows, width), BF16),
+            pltpu.VMEM((width, width), F32),
+            pltpu.VMEM((rows, width), BF16),
         ),
         in_specs=[anywhere] * 9,
-        out_specs=(anywhere, anywhere),
+        out_specs=(pl.BlockSpec(memory_space=pltpu.VMEM),)*2,
         scratch_shapes=[
             vmem(features.shape, BF16),
             vmem(initial.shape, BF16),
@@ -347,16 +395,18 @@
             vmem((batch, width), BF16),
             vmem((members - 1, batch // members, width), BF16),
             vmem((rows, width), F32),
-            vmem((rows, width), BF16),
+            vmem((batch, width), F32),
+            vmem((batch, width), F32),
+            vmem((members - 1, batch, pull // members), BF16),
             vmem((width, width), wire),
             vmem((plane - 1, depth, width), wire),
             vmem((depth, width), wire),
             vmem((planes, depth, width), wire),
             vmem((depth, width), wire),
             vmem((plane, depth, width), wire),
-            vmem((width, width), F32),
             dma((9,)),
-            dma((2,)),
+            pltpu.SemaphoreType.REGULAR,
+            pltpu.SemaphoreType.REGULAR((2, 2)),
             dma((members - 1,)),
             dma((members - 1,)),
             dma((members - 1,)),
@@ -369,7 +419,7 @@
             dma((plane - 1,)),
         ],
         compiler_params=pltpu.CompilerParams(
-            collective_id=0, has_side_effects=True, vmem_limit_bytes=60 * 1024 * 1024
+            collective_id=0, has_side_effects=True, vmem_limit_bytes=62 * 1024 * 1024
         ),
     )(
         features,

time: 26.6 us -> 24.1 us (0.906)
  Pallas kernels: 23.2 us -> 21.8 us
  local copies, waits for them, and re-layouts: 2.52 us -> 1.5 us
    pallas_call x1, Pallas kernels: 23.2 us -> 21.8 us  [local(): pl.pallas_call(functools.partial(kernel, groups, members, low, factor), o...]
    unnamed x4 -> x2, local copies, waits for them, and re-layouts: 2.52 us -> 1.5 us
where the time goes in v2:
time: 24.1 us; the launch traced here: 23.9 us
  Pallas kernels  21.8 us (90%)
  local copies, waits for them, and re-layouts  1.5 us (6%)
  between operations  0.64 us (3%)
    pallas_call x1, Pallas kernels, local(): pl.pallas_call(functools.partial(kernel, groups, members, low, factor), o...  21.8 us
    unnamed x2, local copies, waits for them, and re-layouts  1.5 us

profile of v2, /device:TPU:0, one launch (start us, length us, event | category | flops | bytes accessed | tf_op | source)
XLA Modules:
  0.0 23.9 jit_solution(17670765776717235170)
XLA Ops:
  0.6 21.8 %shard_map.104 = (f32[256,256]{1,0:T(8,128)S(1)}, bf16[1024,256]{1,0:T(8,128)(2,1)S(1)}) custom-call(bf16[512,256]{1,0:T(8,128)(2,1)} %features_in.1, bf16[512,256]{1,0:T(8,128)(2,1)} %initial_in.1, bf16[256,256]{1,0:T(8,128)(2,1)} %weight_in.1, s32[512,512]{1,0:T(8,128)} %mask_in_in.1, s32[512,512]{1,0:T(8,128)} %mask_out_in.1, ...), custom_call_target="tpu_custom_call" | custom-call | tf_op jit(solution)/shard_map/pallas_call | solution.py:375
  22.4 0.7 %copy.13 = f32[256,256]{1,0:T(8,128)} copy(f32[256,256]{1,0:T(8,128)S(1)} %get-tuple-element.2) | data formatting | bytes 524288
  23.1 0.8 %copy.14 = bf16[1024,256]{1,0:T(8,128)(2,1)} copy(bf16[1024,256]{1,0:T(8,128)(2,1)S(1)} %get-tuple-element.3) | data formatting | bytes 1048576

commit v3 on v2

--- a/solution.py
+++ b/solution.py
@@ -151,10 +151,14 @@
         )
     ):
         loads[name] = pltpu.make_async_copy(src, dst, load_sem.at[i])
-        loads[name].start()
+        if name in ("serve", "history"):
+            loads[name].start()
 
     loads["serve"].wait()
     loads["history"].wait()
+    for name in loads:
+        if name not in ("serve", "history"):
+            loads[name].start()
 
     def gather(j):
         wanted = serve[:, pl.ds(pl.multiple_of(j * k, 128), k)]

time: 24.1 us -> 24.1 us (level)
  no operation moved by 1% of the time
where the time goes in v3:
time: 24.1 us; the launch traced here: 23.9 us
  Pallas kernels  21.8 us (90%)
  local copies, waits for them, and re-layouts  1.5 us (6%)
  between operations  0.64 us (3%)
    pallas_call x1, Pallas kernels, local(): pl.pallas_call(functools.partial(kernel, groups, members, low, factor), o...  21.8 us
    unnamed x2, local copies, waits for them, and re-layouts  1.5 us

profile of v3, /device:TPU:0, one launch (start us, length us, event | category | flops | bytes accessed | tf_op | source)
XLA Modules:
  0.0 23.9 jit_solution(10184963151909292575)
XLA Ops:
  0.6 21.8 %shard_map.104 = (f32[256,256]{1,0:T(8,128)S(1)}, bf16[1024,256]{1,0:T(8,128)(2,1)S(1)}) custom-call(bf16[512,256]{1,0:T(8,128)(2,1)} %features_in.1, bf16[512,256]{1,0:T(8,128)(2,1)} %initial_in.1, bf16[256,256]{1,0:T(8,128)(2,1)} %weight_in.1, s32[512,512]{1,0:T(8,128)} %mask_in_in.1, s32[512,512]{1,0:T(8,128)} %mask_out_in.1, ...), custom_call_target="tpu_custom_call" | custom-call | tf_op jit(solution)/shard_map/pallas_call | solution.py:379
  22.4 0.7 %copy.13 = f32[256,256]{1,0:T(8,128)} copy(f32[256,256]{1,0:T(8,128)S(1)} %get-tuple-element.2) | data formatting | bytes 524288
  23.1 0.8 %copy.14 = bf16[1024,256]{1,0:T(8,128)(2,1)} copy(bf16[1024,256]{1,0:T(8,128)(2,1)S(1)} %get-tuple-element.3) | data formatting | bytes 1048576
